TPU v7x, 128 devices: a whole 4x4x4 slice. The times are simulated.
128 devices in a mesh: freq: 8 (over z_lo, y), pts: 16 (over z_hi, x, core).
Axes of the slice: x: 4, y: 4, z: 4 (z_hi: 2, z_lo: 2; z = z_hi * 2 + z_lo), core: 2. Of those that a mesh axis runs over, the one named last changes fastest.
Arguments:
- orbitals: bfloat16 [16384, 512], P('pts'), may hold values from -6 to 6
- energies: float32 [512], replicated, may hold values from -1 to 1
- freq_nodes: float32 [16], P('freq'), may hold values from 0.05 to 4
- weights_q: float32 [16], P('freq'), may hold values from 0.02 to 0.2
- screened: bfloat16 [8192, 16, 4096], P('pts', 'freq'), may hold values from -0.0014648438 to 0.0014648438
- tile_rows: int32 [8192], P('pts'), may hold values from 0 to 15
- tile_cols: int32 [8192], P('pts'), may hold values from 0 to 255, as said below
- tile_count: int32 [16], P('pts'), may hold values from 64 to 512, as said below
Outputs:
- sigma: float32 [512], replicated
Inputs may be any that keep to these rules, and one draw needn't show every extreme that they name: Each group's live slots are its first tile_count slots; one group has exactly 512. `tile_cols`: A slot's column tile lies within 16 tiles of its global row tile.
All inputs are finite; a program needn't handle non-finite values.
Results may differ from a plain program's by a relative error of at most 0.0045.
Values may be sent and summed in bfloat16 or wider, within the bound.
No kernel may reach another device: no remote copies, remote signals or barrier semaphores. Data moves between devices by JAX's collectives and lax.ppermute only.
A program may use at most 64 MiB of HBM per device.

v0:
```python
import jax
import jax.numpy as jnp
from jax import lax
from jax.sharding import PartitionSpec as P

ORBS = 512
TILE = 64


def padded(cells, sides, width):
    for axis, dim in sides:
        count = lax.axis_size(axis)
        ends = count - 1
        head = lax.slice_in_dim(cells, 0, width, axis=dim)
        tail = lax.slice_in_dim(cells, cells.shape[dim] - width, cells.shape[dim], axis=dim)
        cells = jnp.concatenate(
            [
                lax.ppermute(tail, axis, [(i, (i + 1) % count) for i in range(ends)]),
                cells,
                lax.ppermute(head, axis, [((i + 1) % count, i) for i in range(ends)]),
            ],
            axis=dim,
        )
    return cells


def tile_pass(
    running,
    ordering,
    count,
    left_table,
    left_offset,
    right_table,
    right_offset,
    row_index,
    col_index,
    tile_data,
    green_weight,
    weights_q,
    block_size,
):
    slot_total = ordering.shape[0]
    freq_here = tile_data.shape[1]
    block_count = (count + block_size - 1) // block_size

    def advance(block_id, total):
        offsets = block_id * block_size + jnp.arange(block_size, dtype=jnp.int32)
        usable = offsets < count
        chosen = ordering[jnp.minimum(offsets, slot_total - 1)]
        tiles = tile_data[chosen]
        left = left_table[row_index[chosen] - left_offset]
        right = right_table[col_index[chosen] - right_offset]
        for freq_id in range(freq_here):
            scaled = (right * green_weight[freq_id]).astype(jnp.bfloat16)
            green = jnp.einsum("tim,tjm->tij", left, scaled, preferred_element_type=jnp.float32)
            product = (green * tiles[:, freq_id].reshape(block_size, TILE, TILE)).astype(
                jnp.bfloat16
            )
            image = jnp.einsum("tij,tjm->tim", product, right, preferred_element_type=jnp.float32)
            terms = jnp.where(usable[:, None, None], left * image, 0.0)
            total = total + weights_q[freq_id] * jnp.sum(terms, axis=(0, 1))
        return total

    return lax.fori_loop(0, block_count, advance, running)


def body(orbitals, energies, freq_nodes, weights_q, screened, tile_rows, tile_cols, tile_count):
    position = lax.axis_index("pts")
    slot_total = screened.shape[0]
    rows_here = orbitals.shape[0]
    row_blocks = rows_here // TILE
    global_rows = position * row_blocks + tile_rows
    green_weight = energies[None, :] / (energies[None, :] ** 2 + freq_nodes[:, None] ** 2)
    live_total = tile_count[0]
    block_size = min(64, slot_total)
    running = jnp.zeros((ORBS,), jnp.float32)
    widened = padded(orbitals, (("pts", 0),), rows_here)
    orbital_table = widened.reshape(-1, TILE, ORBS)
    row_offset = (position - 1) * row_blocks
    ordering = jnp.arange(slot_total, dtype=jnp.int32)
    running = tile_pass(
        running,
        ordering,
        live_total,
        orbital_table,
        row_offset,
        orbital_table,
        row_offset,
        global_rows,
        tile_cols,
        screened,
        green_weight,
        weights_q,
        block_size,
    )
    total = lax.psum(running, ("freq", "pts"))
    return -total


def solution(mesh):
    placed = (
        P("pts", None),
        P(),
        P("freq"),
        P("freq"),
        P("pts", "freq", None),
        P("pts"),
        P("pts"),
        P("pts"),
    )
    return jax.shard_map(body, mesh=mesh, in_specs=placed, out_specs=P(), check_vma=False)
```

profile of v0, /device:TPU:0, one launch (start us, length us, event | category | flops | bytes accessed | tf_op | source)
XLA Modules:
  0.0 491.6 jit_solution(5776854961972201026)
XLA Ops:
  0.0 1.5 collective-permute-start
  1.5 1.3 collective-permute-start.1
  3.5 0.8 integer_pow.8
  4.2 0.7 integer_pow.9
  5.0 0.7 broadcast_add_fusion
  5.6 0.8 add_divide_fusion
  6.4 1.0 copy-done.1
  7.4 0.7 collective-permute-done.1
  8.1 2.0 pad_maximum_fusion
  10.1 202.0 %while.11 = (s32[]{:T(128)}, f32[512]{0:T(512)S(1)}, s32[]{:T(128)}, f32[2]{0:T(128)S(1)}, s32[]{:T(128)}, /*index=5*/s32[512]{0:T(512)S(1)}, s32[]{:T(128)}, bf...) while((s32[]{:T(128)}, f32[512]{0:T(512)S(1)}, ...), condition=%wide.region_3.4_spmd.clone, body=%wide.region_0.3_spmd.clone.sunk | while | flops 1104681088 | bytes 45138032 | solution.py:64
  10.2 0.8 gather_fusion
  11.0 0.8 gather_fusion.1
  11.8 0.8 gather_fusion.2
  12.6 2.7 gather_fusion.3
  15.4 2.8 gather_fusion.4
  18.2 7.0 %gather_fusion.5 = bf16[64,2,4096]{2,1,0:T(2,128)(2,1)} fusion(bf16[512,2,4096]{2,1,0:T(2,128)(2,1)} %get-tuple-element.244, s32[1024]{0:T(1024)S(1)} %pad_clamp_fusion.9), kind=kCustom, calls=%fused_computation.5.clone.clone.1 | custom fusion | bytes 2097408 | tf_op jit(solution)/shard_map/while/body/gather | solution.py:50
  25.2 8.9 %fusion.57 = (f32[64,4096]{1,0:T(8,128)}, f32[64,4096]{1,0:T(8,128)}) fusion(bf16[64,2,4096]{2,1,0:T(2,128)(2,1)} %gather_fusion.5), kind=kLoop, calls=%fused_computation.26.clone.1 | loop fusion | flops 524288 | bytes 3145728 | tf_op jit(solution)/shard_map/while/body/convert_element_type | solution.py:56
  34.1 3.2 reshape.185
  37.3 0.7 add_compare_fusion.2
  37.9 8.8 %fusion.60 = f32[512]{0:T(512)S(1)} fusion(bf16[64,64,512]{2,1,0:T(8,128)(2,1)} %gather_fusion.3, pred[64]{0:T(512)(128)(4,1)S(1)} %add_compare_fusion.2, bf16[64,64,512]{2,1,0:T(8,128)(2,1)} %gather_fusion.4, f32[64,64,64]{2,1,0:T(8,128)} %reshape.185, f32[512]{0:T(512)S(1)} %bitcast.53), kind=kOutput, calls=%fused_computation.12.clone.1 | convolution fusion | flops 552074752 | bytes 9441344 | tf_op jit(solution)/shard_map/while/body/tij,tjm->tim/dot_general | solution.py:59
  46.8 3.2 reshape.184
  49.9 8.8 %fusion.59 = f32[512]{0:T(512)S(1)} fusion(bf16[64,64,512]{2,1,0:T(8,128)(2,1)} %gather_fusion.3, pred[64]{0:T(512)(128)(4,1)S(1)} %add_compare_fusion.2, bf16[64,64,512]{2,1,0:T(8,128)(2,1)} %gather_fusion.4, f32[64,64,64]{2,1,0:T(8,128)} %reshape.184, f32[512]{0:T(512)S(1)} %bitcast.52), kind=kOutput, calls=%fused_computation.14.clone.1 | convolution fusion | flops 552074752 | bytes 9441344 | tf_op jit(solution)/shard_map/while/body/tij,tjm->tim/dot_general | solution.py:59
  58.8 0.6 fusion.61
  59.4 1.3 multiply_add_fusion.2
  60.7 0.8 gather_fusion
  61.5 0.8 gather_fusion.1
  62.3 0.8 gather_fusion.2
  63.1 2.7 gather_fusion.3
  65.9 2.8 gather_fusion.4
  68.7 7.0 %gather_fusion.5 = bf16[64,2,4096]{2,1,0:T(2,128)(2,1)} fusion(bf16[512,2,4096]{2,1,0:T(2,128)(2,1)} %get-tuple-element.244, s32[1024]{0:T(1024)S(1)} %pad_clamp_fusion.9), kind=kCustom, calls=%fused_computation.5.clone.clone.1 | custom fusion | bytes 2097408 | tf_op jit(solution)/shard_map/while/body/gather | solution.py:50
  75.7 8.9 %fusion.57 = (f32[64,4096]{1,0:T(8,128)}, f32[64,4096]{1,0:T(8,128)}) fusion(bf16[64,2,4096]{2,1,0:T(2,128)(2,1)} %gather_fusion.5), kind=kLoop, calls=%fused_computation.26.clone.1 | loop fusion | flops 524288 | bytes 3145728 | tf_op jit(solution)/shard_map/while/body/convert_element_type | solution.py:56
  84.6 3.2 reshape.185
  87.8 0.7 add_compare_fusion.2
  88.4 8.8 %fusion.60 = f32[512]{0:T(512)S(1)} fusion(bf16[64,64,512]{2,1,0:T(8,128)(2,1)} %gather_fusion.3, pred[64]{0:T(512)(128)(4,1)S(1)} %add_compare_fusion.2, bf16[64,64,512]{2,1,0:T(8,128)(2,1)} %gather_fusion.4, f32[64,64,64]{2,1,0:T(8,128)} %reshape.185, f32[512]{0:T(512)S(1)} %bitcast.53), kind=kOutput, calls=%fused_computation.12.clone.1 | convolution fusion | flops 552074752 | bytes 9441344 | tf_op jit(solution)/shard_map/while/body/tij,tjm->tim/dot_general | solution.py:59
  97.3 3.2 reshape.184
  100.4 8.8 %fusion.59 = f32[512]{0:T(512)S(1)} fusion(bf16[64,64,512]{2,1,0:T(8,128)(2,1)} %gather_fusion.3, pred[64]{0:T(512)(128)(4,1)S(1)} %add_compare_fusion.2, bf16[64,64,512]{2,1,0:T(8,128)(2,1)} %gather_fusion.4, f32[64,64,64]{2,1,0:T(8,128)} %reshape.184, f32[512]{0:T(512)S(1)} %bitcast.52), kind=kOutput, calls=%fused_computation.14.clone.1 | convolution fusion | flops 552074752 | bytes 9441344 | tf_op jit(solution)/shard_map/while/body/tij,tjm->tim/dot_general | solution.py:59
  109.9 1.3 multiply_add_fusion.2
  111.2 0.8 gather_fusion
  112.0 0.8 gather_fusion.1
  112.8 0.8 gather_fusion.2
  113.6 2.7 gather_fusion.3
  116.4 2.8 gather_fusion.4
  119.2 7.0 %gather_fusion.5 = bf16[64,2,4096]{2,1,0:T(2,128)(2,1)} fusion(bf16[512,2,4096]{2,1,0:T(2,128)(2,1)} %get-tuple-element.244, s32[1024]{0:T(1024)S(1)} %pad_clamp_fusion.9), kind=kCustom, calls=%fused_computation.5.clone.clone.1 | custom fusion | bytes 2097408 | tf_op jit(solution)/shard_map/while/body/gather | solution.py:50
  126.2 8.9 %fusion.57 = (f32[64,4096]{1,0:T(8,128)}, f32[64,4096]{1,0:T(8,128)}) fusion(bf16[64,2,4096]{2,1,0:T(2,128)(2,1)} %gather_fusion.5), kind=kLoop, calls=%fused_computation.26.clone.1 | loop fusion | flops 524288 | bytes 3145728 | tf_op jit(solution)/shard_map/while/body/convert_element_type | solution.py:56
  135.1 3.2 reshape.185
  138.3 0.7 add_compare_fusion.2
  138.9 8.8 %fusion.60 = f32[512]{0:T(512)S(1)} fusion(bf16[64,64,512]{2,1,0:T(8,128)(2,1)} %gather_fusion.3, pred[64]{0:T(512)(128)(4,1)S(1)} %add_compare_fusion.2, bf16[64,64,512]{2,1,0:T(8,128)(2,1)} %gather_fusion.4, f32[64,64,64]{2,1,0:T(8,128)} %reshape.185, f32[512]{0:T(512)S(1)} %bitcast.53), kind=kOutput, calls=%fused_computation.12.clone.1 | convolution fusion | flops 552074752 | bytes 9441344 | tf_op jit(solution)/shard_map/while/body/tij,tjm->tim/dot_general | solution.py:59
  147.8 3.2 reshape.184
  150.9 8.8 %fusion.59 = f32[512]{0:T(512)S(1)} fusion(bf16[64,64,512]{2,1,0:T(8,128)(2,1)} %gather_fusion.3, pred[64]{0:T(512)(128)(4,1)S(1)} %add_compare_fusion.2, bf16[64,64,512]{2,1,0:T(8,128)(2,1)} %gather_fusion.4, f32[64,64,64]{2,1,0:T(8,128)} %reshape.184, f32[512]{0:T(512)S(1)} %bitcast.52), kind=kOutput, calls=%fused_computation.14.clone.1 | convolution fusion | flops 552074752 | bytes 9441344 | tf_op jit(solution)/shard_map/while/body/tij,tjm->tim/dot_general | solution.py:59
  160.4 1.3 multiply_add_fusion.2
  161.7 0.8 gather_fusion
  162.5 0.8 gather_fusion.1
  163.3 0.8 gather_fusion.2
  164.1 2.7 gather_fusion.3
  166.9 2.8 gather_fusion.4
  169.6 7.0 %gather_fusion.5 = bf16[64,2,4096]{2,1,0:T(2,128)(2,1)} fusion(bf16[512,2,4096]{2,1,0:T(2,128)(2,1)} %get-tuple-element.244, s32[1024]{0:T(1024)S(1)} %pad_clamp_fusion.9), kind=kCustom, calls=%fused_computation.5.clone.clone.1 | custom fusion | bytes 2097408 | tf_op jit(solution)/shard_map/while/body/gather | solution.py:50
  176.7 8.9 %fusion.57 = (f32[64,4096]{1,0:T(8,128)}, f32[64,4096]{1,0:T(8,128)}) fusion(bf16[64,2,4096]{2,1,0:T(2,128)(2,1)} %gather_fusion.5), kind=kLoop, calls=%fused_computation.26.clone.1 | loop fusion | flops 524288 | bytes 3145728 | tf_op jit(solution)/shard_map/while/body/convert_element_type | solution.py:56
  185.6 3.2 reshape.185
  188.8 0.7 add_compare_fusion.2
  189.4 8.8 %fusion.60 = f32[512]{0:T(512)S(1)} fusion(bf16[64,64,512]{2,1,0:T(8,128)(2,1)} %gather_fusion.3, pred[64]{0:T(512)(128)(4,1)S(1)} %add_compare_fusion.2, bf16[64,64,512]{2,1,0:T(8,128)(2,1)} %gather_fusion.4, f32[64,64,64]{2,1,0:T(8,128)} %reshape.185, f32[512]{0:T(512)S(1)} %bitcast.53), kind=kOutput, calls=%fused_computation.12.clone.1 | convolution fusion | flops 552074752 | bytes 9441344 | tf_op jit(solution)/shard_map/while/body/tij,tjm->tim/dot_general | solution.py:59
  198.3 3.2 reshape.184
  201.4 8.8 %fusion.59 = f32[512]{0:T(512)S(1)} fusion(bf16[64,64,512]{2,1,0:T(8,128)(2,1)} %gather_fusion.3, pred[64]{0:T(512)(128)(4,1)S(1)} %add_compare_fusion.2, bf16[64,64,512]{2,1,0:T(8,128)(2,1)} %gather_fusion.4, f32[64,64,64]{2,1,0:T(8,128)} %reshape.184, f32[512]{0:T(512)S(1)} %bitcast.52), kind=kOutput, calls=%fused_computation.14.clone.1 | convolution fusion | flops 552074752 | bytes 9441344 | tf_op jit(solution)/shard_map/while/body/tij,tjm->tim/dot_general | solution.py:59
  210.9 1.3 multiply_add_fusion.2
  212.1 278.8 %psum.7 = f32[512]{0:T(512)S(1)} all-reduce(f32[512]{0:T(512)S(1)} %get-tuple-element.68), channel_id=1, replica_groups=mesh['freq'=8,'pts'=16] {'freq','pts'}, use_global_device_ids=true, to_apply=%region_4.5 | all-reduce | flops 512 | bytes 4096 | tf_op jit(solution)/shard_map/psum | solution.py:96
  (47 shorter events, 2.6 us)
Async XLA Ops:
  0.0 10.1 %copy-start.2 = (f32[2]{0:T(128)S(1)}, f32[2]{0:T(128)}, u32[]{:S(2)}) copy-start(f32[2]{0:T(128)} %param.13) | copy-start | bytes 28
  0.0 10.1 %copy-start = (s32[512]{0:T(512)S(1)}, s32[512]{0:T(512)}, u32[]{:S(2)}) copy-start(s32[512]{0:T(512)} %param.16) | copy-start | bytes 6148
  0.0 6.4 %collective-permute-start = (bf16[1024,512]{1,0:T(8,128)(2,1)}, bf16[1024,512]{1,0:T(8,128)(2,1)S(1)}, u32[]{:S(2)}, u32[]{:S(2)}) collective-permute-start(bf16[1024,512]{1,0:T(8,128)(2,1)} %param.10), channel_id=1, source_target_pairs={{0,1},{1,2},{2,3},{3,4},{4,5},{5,6},{6,7},{7,8},{8,9},{9,10},{10,1... | collective-permute-start | bytes 3145736 | tf_op jit(solution)/shard_map/ppermute | solution.py:18
  1.5 6.6 %collective-permute-start.1 = (bf16[1024,512]{1,0:T(8,128)(2,1)}, bf16[1024,512]{1,0:T(8,128)(2,1)}, u32[]{:S(2)}, u32[]{:S(2)}) collective-permute-start(bf16[1024,512]{1,0:T(8,128)(2,1)} %param.10), channel_id=1, source_target_pairs={{1,0},{2,1},{3,2},{4,3},{5,4},{6,5},{7,6},{8,7},{9,8},{10,9},{11,1... | collective-permute-start | bytes 3145736 | tf_op jit(solution)/shard_map/ppermute | solution.py:20
  6.4 1.0 copy-start.1
where the time goes:
time: 494 us; the launch traced here: 492 us
  blocking collectives  279 us (56%)
  local copies, waits for them, and re-layouts  88.6 us (18%)
  matrix products  70.7 us (14%)
  other arithmetic  49 us (10%)
    psum x1, blocking collectives, body(): total = lax.psum(running, ('freq', 'pts'))  279 us
    dot_general x8, matrix products, advance(): jnp.einsum('tij,tjm->tim', product, right, preferred_element_type=jnp.flo...  70.7 us
    convert_element_type x4, other arithmetic, advance(): green * tiles[:, freq_id].reshape(block_size, TILE, TILE)  35.6 us
    gather x4, local copies, waits for them, and re-layouts, advance(): tiles = tile_data[chosen]  28.1 us
    convert_element_type x8, local copies, waits for them, and re-layouts, advance(): green * tiles[:, freq_id].reshape(block_size, TILE, TILE)  25.3 us
    gather x8, local copies, waits for them, and re-layouts, advance(): right = right_table[col_index[chosen] - right_offset]  14.3 us
    gather x8, local copies, waits for them, and re-layouts, advance(): left = left_table[row_index[chosen] - left_offset]  14.1 us
  transfers between devices with their start and end apart: 2, of which 1 were waited for; matrix products, arithmetic and copies ran while one was open for 1% of the time, Pallas kernels for 0%

commit v1 on v0

v1 whole, which is shorter than its diff:
```python
import jax
import jax.numpy as jnp
from jax import lax
from jax.experimental import pallas as pl
from jax.experimental.pallas import tpu as pltpu
from jax.sharding import PartitionSpec as P

ORBS = 512
TILE = 64
HALF = 32
BAND = 16
BLOCK = 4
SPAN = BLOCK * TILE
BLOCKS = BAND // BLOCK
CHUNK = 64

F32 = jnp.float32
BF16 = jnp.bfloat16


def weight_row(energies, node):
    return energies / (energies * energies + node * node)


def scale_into(scaled, points, energies_ref, nodes_ref):
    for f in range(2):
        weight = weight_row(energies_ref[...], nodes_ref[f])
        scaled[f] = (points[...].astype(F32) * weight).astype(BF16)


def block_terms(rows, cols_scaled, cols, w_of, ratio):
    dims = (((1,), (1,)), ((), ()))
    g0 = lax.dot_general(rows, cols_scaled(0), dims, preferred_element_type=F32)
    g1 = lax.dot_general(rows, cols_scaled(1), dims, preferred_element_type=F32)
    product = g0 * w_of(0).astype(F32) + ratio * (g1 * w_of(1).astype(F32))
    image = jnp.dot(product.astype(BF16), cols(), preferred_element_type=F32)
    return jnp.sum(image * rows.astype(F32), axis=0, keepdims=True)


def own_kernel(
    count_ref,
    rows_ref,
    cols_ref,
    nodes_ref,
    weights_ref,
    orb_ref,
    energies_ref,
    screened_ref,
    sigma_ref,
    perm_ref,
    halo_ref,
    raw,
    dense,
    sorted_w,
    scaled,
    wide,
    raw_sem,
    out_sem,
):
    slots = screened_ref.shape[0]
    chunks = slots // CHUNK
    count = count_ref[0]
    first = (lax.axis_index("pts") - 1) * BAND

    def fetch(k):
        part = pl.ds(k * CHUNK, CHUNK)
        return pltpu.make_async_copy(screened_ref.at[part], raw.at[part], raw_sem.at[k])

    for k in range(chunks):

        @pl.when(k * CHUNK < count)
        def _():
            fetch(k).start()

    for q in range(ORBS // 128):
        lanes = pl.ds(q * 128, 128)
        wide[q] = orb_ref[:, lanes].astype(F32)
        for b in range(BLOCKS):
            for h in range(2):
                perm_ref[pl.ds(b * SPAN + h * SPAN // 2, SPAN // 2), lanes] = wide[
                    q, pl.ds(b * SPAN + h, SPAN // 2, stride=2), :
                ].astype(BF16)
    scale_into(scaled, orb_ref, energies_ref, nodes_ref)

    def clear(r, carry):
        dense[:, r] = jnp.zeros(dense.shape[:1] + dense.shape[2:], F32)
        return carry

    lax.fori_loop(0, BAND, clear, 0)

    def place(s):
        return rows_ref[s], cols_ref[s] - first

    def values(s):
        return raw[s].astype(F32).reshape(2, HALF, 2 * TILE)

    def scatter(s):
        r, c = place(s)
        dense[:, r, c] = dense[:, r, c] + values(s)

    def scatter_two(s):
        r0, c0 = place(s)
        r1, c1 = place(s + 1)
        same = ((r0 == r1) & (c0 == c1)).astype(jnp.int32).astype(F32)
        x0 = values(s)
        x1 = values(s + 1)
        old0 = dense[:, r0, c0]
        old1 = dense[:, r1, c1]
        dense[:, r0, c0] = old0 + x0
        dense[:, r1, c1] = old1 + (x1 + same * x0)

    for k in range(chunks):

        @pl.when(k * CHUNK < count)
        def _():
            fetch(k).wait()
            here = jnp.minimum(count - k * CHUNK, CHUNK)

            def two(i, carry):
                scatter_two(k * CHUNK + 2 * i)
                return carry

            lax.fori_loop(0, here // 2, two, 0)

            @pl.when(here % 2 == 1)
            def _():
                scatter(k * CHUNK + here - 1)

    low = lax.broadcasted_iota(jnp.int32, (SPAN // 2, 2 * TILE), 1) < TILE

    def arrange(side, f, b, pair):
        parts = []
        for d in range(2):
            c = side * BAND + 2 * pair + d
            parts.append(dense[f, pl.ds(b * BLOCK, BLOCK), c].reshape(SPAN // 2, 2 * TILE))
        v0, v1 = parts
        even = jnp.where(low, v0, pltpu.roll(v1, TILE, 1))
        odd = jnp.where(low, pltpu.roll(v0, TILE, 1), v1)
        lanes = pl.ds(pair * 2 * TILE, 2 * TILE)
        sorted_w[side, f, pl.ds(b * SPAN, SPAN // 2), lanes] = even.astype(BF16)
        sorted_w[side, f, pl.ds(b * SPAN + SPAN // 2, SPAN // 2), lanes] = odd.astype(BF16)

    def arrange_block(side, b, c):
        for f in range(2):
            for pair in range(2 * c, 2 * c + 2):
                arrange(side, f, b, pair)

    outs = [
        pltpu.make_async_copy(sorted_w.at[2 * k], halo_ref.at[k], out_sem.at[k]) for k in range(2)
    ]
    for b in range(BLOCKS):
        for c in range(BLOCKS):
            if c >= b:
                arrange_block(0, b, c)
            if c <= b:
                arrange_block(2, b, c)
    for copy in outs:
        copy.start()
    ratio = weights_ref[1] / weights_ref[0]
    total = jnp.zeros((1, ORBS), F32)
    for b in range(BLOCKS):
        for c in range(BLOCKS):
            arrange_block(1, b, c)
        total += block_terms(
            perm_ref[pl.ds(b * SPAN, SPAN), :],
            lambda f: scaled[f],
            lambda: orb_ref[...],
            lambda f: sorted_w[1, f, pl.ds(b * SPAN, SPAN), :],
            ratio,
        )
    sigma_ref[...] = -weights_ref[0] * total
    for copy in outs:
        copy.wait()


def own_part(count, rows, cols, nodes, weights, orbitals, energies, screened):
    points = orbitals.shape[0]
    smem = pl.BlockSpec(memory_space=pltpu.SMEM)
    vmem = pl.BlockSpec(memory_space=pltpu.VMEM)
    hbm = pl.BlockSpec(memory_space=pl.ANY)
    return pl.pallas_call(
        own_kernel,
        out_shape=(
            jax.ShapeDtypeStruct((1, ORBS), F32),
            jax.ShapeDtypeStruct((points, ORBS), BF16),
            jax.ShapeDtypeStruct((2, 2, points, points), BF16),
        ),
        in_specs=[smem] * 5 + [vmem, vmem, hbm],
        out_specs=(vmem, vmem, hbm),
        scratch_shapes=[
            pltpu.VMEM(screened.shape, BF16),
            pltpu.VMEM((2, BAND, 3 * BAND, HALF, 2 * TILE), F32),
            pltpu.VMEM((3, 2, points, points), BF16),
            pltpu.VMEM((2, points, ORBS), BF16),
            pltpu.VMEM((ORBS // 128, points, 128), F32),
            pltpu.SemaphoreType.DMA((screened.shape[0] // CHUNK,)),
            pltpu.SemaphoreType.DMA((2,)),
        ],
        compiler_params=pltpu.CompilerParams(vmem_limit_bytes=58 << 20),
    )(count, rows, cols, nodes, weights, orbitals, energies, screened)


def halo_kernel(
    side_ref,
    nodes_ref,
    weights_ref,
    perm_ref,
    orb_ref,
    energies_ref,
    sigma_in,
    halo_ref,
    sigma_ref,
    tiles,
    scaled,
    sem,
):
    side = side_ref[0]
    copy = pltpu.make_async_copy(halo_ref.at[side], tiles, sem)
    copy.start()
    scale_into(scaled, orb_ref, energies_ref, nodes_ref)
    copy.wait()
    ratio = weights_ref[1] / weights_ref[0]
    total = jnp.zeros((1, ORBS), F32)
    for t in range(BLOCKS):
        width = (BLOCKS - t) * SPAN
        b = t + side * (BLOCKS - 1 - 2 * t)
        rows = pl.ds(pl.multiple_of(b * SPAN, SPAN), SPAN)
        lead = (1 - side) * t
        cols = pl.ds(pl.multiple_of(lead * SPAN, SPAN), width)
        total += block_terms(
            perm_ref[rows, :],
            lambda f: scaled[f, cols, :],
            lambda: orb_ref[cols, :],
            lambda f: tiles[f, rows, cols],
            ratio,
        )
    sigma_ref[...] = sigma_in[...] - weights_ref[0] * total


def halo_part(side, nodes, weights, perm, orbitals, energies, sigma, halo):
    points = orbitals.shape[0]
    smem = pl.BlockSpec(memory_space=pltpu.SMEM)
    vmem = pl.BlockSpec(memory_space=pltpu.VMEM)
    hbm = pl.BlockSpec(memory_space=pl.ANY)
    return pl.pallas_call(
        halo_kernel,
        out_shape=jax.ShapeDtypeStruct((1, ORBS), F32),
        in_specs=[smem] * 3 + [vmem] * 4 + [hbm],
        out_specs=vmem,
        scratch_shapes=[
            pltpu.VMEM(halo.shape[1:], BF16),
            pltpu.VMEM((2, points, ORBS), BF16),
            pltpu.SemaphoreType.DMA,
        ],
        compiler_params=pltpu.CompilerParams(vmem_limit_bytes=58 << 20),
    )(side, nodes, weights, perm, orbitals, energies, sigma, halo)


AXES = ("freq", "pts")


def device(f, p):
    return f * 16 + p


def inner_pairs():
    return [(device(f, p), device(f, p ^ 1)) for f in range(8) for p in range(16)]


def outer_pairs():
    pairs = []
    for f in range(8):
        for p in range(1, 15, 2):
            to = device(f ^ 4 if p == 7 else f, p + 1)
            pairs += [(device(f, p), to), (to, device(f, p))]
    return pairs


def total_over_devices(x):
    for mask in (1, 2, 6, 64, 72, 16, 48):
        x = x + lax.ppermute(x, AXES, [(i, i ^ mask) for i in range(128)])
    return x


def body(orbitals, energies, freq_nodes, weights_q, screened, tile_rows, tile_cols, tile_count):
    position = lax.axis_index("pts")
    outer = lax.ppermute(orbitals, AXES, outer_pairs())
    inner = lax.ppermute(orbitals, AXES, inner_pairs())
    energies = energies[None, :]
    sigma, perm, halo = own_part(
        tile_count, tile_rows, tile_cols, freq_nodes, weights_q, orbitals, energies, screened
    )
    odd = (position % 2).astype(jnp.int32)
    for side, points in ((1 - odd, inner), (odd, outer)):
        sigma = halo_part(
            side[None], freq_nodes, weights_q, perm, points, energies, sigma, halo
        )
    return total_over_devices(sigma[0])


def solution(mesh):
    placed = (
        P("pts", None),
        P(),
        P("freq"),
        P("freq"),
        P("pts", "freq", None),
        P("pts"),
        P("pts"),
        P("pts"),
    )
    return jax.shard_map(body, mesh=mesh, in_specs=placed, out_specs=P(), check_vma=False)
```

time: 494 us -> 70.6 us (0.14)
  blocking collectives: 279 us -> 0 us
  local copies, waits for them, and re-layouts: 88.6 us -> 1.89 us
  matrix products: 70.7 us -> 0 us
  other arithmetic: 49 us -> 1.28 us
  Pallas kernels: 0 us -> 28.8 us
  starting transfers between devices: 2.77 us -> 24.2 us
  waiting for transfers between devices: 0.7 us -> 13.9 us
    psum x1 -> x0, blocking collectives: 279 us -> none  [body(): total = lax.psum(running, ('freq', 'pts'))]
    dot_general x8 -> x0, matrix products: 70.7 us -> none  [advance(): jnp.einsum('tij,tjm->tim', product, right, preferred_element_type=jnp.flo...]
    gather x24 -> x0, local copies, waits for them, and re-layouts: 59.8 us -> none  [the longest x4 28.1 us: advance(): tiles = tile_data[chosen]]
    convert_element_type x4 -> x0, other arithmetic: 35.6 us -> none  [advance(): green * tiles[:, freq_id].reshape(block_size, TILE, TILE)]
    pallas_call x0 -> x3, Pallas kernels: none -> 28.8 us  [the longest x1 14.9 us: own_part(): pl.pallas_call(own_kernel, out_shape=(jax.ShapeDtypeStruct((1, ORBS), F32...]
    convert_element_type x8 -> x0, local copies, waits for them, and re-layouts: 25.3 us -> none  [advance(): green * tiles[:, freq_id].reshape(block_size, TILE, TILE)]
    ppermute x2 -> x9, starting transfers between devices: 2.77 us -> 24.2 us  [the longest x7 23.4 us: total_over_devices(): x = x + lax.ppermute(x, AXES, [(i, i ^ mask) for i in range(128)])]
    ppermute x2 -> x9, waiting for transfers between devices: 0.7 us -> 13.9 us  [the longest x7 13.9 us: total_over_devices(): x = x + lax.ppermute(x, AXES, [(i, i ^ mask) for i in range(128)])]
  transfers between devices with their start and end apart: 2 -> 9, of which waited for: 1 -> 7; matrix products, arithmetic and copies ran while one was open for 1% -> 0% of each run, Pallas kernels for 0% -> 31%
where the time goes in v1:
time: 70.6 us; the launch traced here: 70.7 us
  Pallas kernels  28.8 us (41%)
  starting transfers between devices  24.2 us (34%)
  waiting for transfers between devices  13.9 us (20%)
  local copies, waits for them, and re-layouts  1.89 us (3%)
  other arithmetic  1.28 us (2%)
  between operations  0.73 us (1%)
    ppermute x7, starting transfers between devices, total_over_devices(): x = x + lax.ppermute(x, AXES, [(i, i ^ mask) for i in range(128)])  23.4 us
    pallas_call x1, Pallas kernels, own_part(): pl.pallas_call(own_kernel, out_shape=(jax.ShapeDtypeStruct((1, ORBS), F32...  14.9 us
    ppermute x7, waiting for transfers between devices, total_over_devices(): x = x + lax.ppermute(x, AXES, [(i, i ^ mask) for i in range(128)])  13.9 us
    pallas_call x2, Pallas kernels, halo_part(): pl.pallas_call(halo_kernel, out_shape=jax.ShapeDtypeStruct((1, ORBS), F32...  13.9 us
    unnamed x4, local copies, waits for them, and re-layouts  1.89 us
  transfers between devices with their start and end apart: 9, of which 7 were waited for; matrix products, arithmetic and copies ran while one was open for 0% of the time, Pallas kernels for 31%

profile of v1, /device:TPU:0, one launch (start us, length us, event | category | flops | bytes accessed | tf_op | source)
XLA Modules:
  0.0 70.7 jit_solution(2988519895106116084)
XLA Ops:
  0.0 0.0 collective-permute-start.1
  0.0 0.7 %collective-permute-start = (bf16[1024,512]{1,0:T(8,128)(2,1)}, bf16[1024,512]{1,0:T(8,128)(2,1)S(1)}, u32[]{:S(2)}, u32[]{:S(2)}) collective-permute-start(bf16[1024,512]{1,0:T(8,128)(2,1)} %orb_ref.1), channel_id=1, source_target_pairs={{1,2},{2,1},{3,4},{4,3},{5,6},{6,5},{7,72},{72,7},{9,10},{10,9},{1... | collective-permute-start | bytes 3145736 | tf_op jit(solution)/shard_map/ppermute | solution.py:287
  1.4 14.9 %shard_map.82 = (f32[1,512]{1,0:T(1,128)}, bf16[1024,512]{1,0:T(8,128)(2,1)}, bf16[2,2,1024,1024]{3,2,1,0:T(8,128)(2,1)}) custom-call(s32[1]{0:T(128)S(6)} %copy.9.count_ref, s32[512]{0:T(512)} %rows_ref.1, s32[512]{0:T(512)} %cols_ref.1, f32[2]{0:T(128)} %nodes_ref.5, f32[2]{0:T(128)} %weights_ref.5, bf16[1024,512]{1,0:T(8,128)(2,1)} %orb_ref.1, ...), custom_call_target="tpu_custom_call" | custom-call | tf_op jit(solution)/shard_map/pallas_call | solution.py:181
  16.3 0.0 collective-permute-done.1.orb_ref
  16.3 0.0 copy-start.1
  16.3 0.9 %copy-done.1 = bf16[1024,512]{1,0:T(8,128)(2,1)} copy-done((bf16[1024,512]{1,0:T(8,128)(2,1)}, bf16[1024,512]{1,0:T(8,128)(2,1)S(1)}, u32[]{:S(2)}) %copy-start.1) | copy-done | bytes 1048600
  17.3 6.9 %shard_map.83.sigma_in = f32[1,512]{1,0:T(1,128)} custom-call(s32[1]{0:T(128)} %bitcast.2.side_ref, f32[2]{0:T(128)} %nodes_ref.5, f32[2]{0:T(128)} %weights_ref.5, bf16[1024,512]{1,0:T(8,128)(2,1)} %get-tuple-element.8.perm_ref, bf16[1024,512]{1,0:T(8,128)(2,1)} %copy-done.1, f32[1,512]{1,0:T(1,128)} %bitcast.5, f32[1,512]{1,0:T(1,128)} %get-tuple-element.9.sigma_in, ...), custom_call_target="tpu_custom_call" | custom-call | tf_op jit(solution)/shard_map/pallas_call | solution.py:245
  24.2 0.0 collective-permute-done.orb_ref
  24.2 0.0 copy-start
  24.2 0.9 %copy-done = bf16[1024,512]{1,0:T(8,128)(2,1)} copy-done((bf16[1024,512]{1,0:T(8,128)(2,1)}, bf16[1024,512]{1,0:T(8,128)(2,1)S(1)}, u32[]{:S(2)}) %copy-start) | copy-done | bytes 1048600
  25.1 7.0 %shard_map.84 = f32[1,512]{1,0:T(1,128)} custom-call(s32[1]{0:T(128)} %bitcast.side_ref, f32[2]{0:T(128)} %nodes_ref.5, f32[2]{0:T(128)} %weights_ref.5, bf16[1024,512]{1,0:T(8,128)(2,1)} %get-tuple-element.8.perm_ref, bf16[1024,512]{1,0:T(8,128)(2,1)} %copy-done, f32[1,512]{1,0:T(1,128)} %bitcast.6, f32[1,512]{1,0:T(1,128)} %shard_map.83.sigma_in, ...), custom_call_target="tpu_custom_call" | custom-call | tf_op jit(solution)/shard_map/pallas_call | solution.py:245
  32.1 4.4 %collective-permute-start.2 = (f32[512]{0:T(512)}, f32[512]{0:T(512)S(1)}, u32[]{:S(2)}, u32[]{:S(2)}) collective-permute-start(f32[512]{0:T(512)} %bitcast.7), channel_id=1, source_target_pairs={{0,1},{1,0},{2,3},{3,2},{4,5},{5,4},{6,7},{7,6},{8,9},{9,8},{10,11... | collective-permute-start | bytes 6152 | tf_op jit(solution)/shard_map/ppermute | solution.py:281
  36.5 1.0 %collective-permute-done.2 = f32[512]{0:T(512)S(1)} collective-permute-done((f32[512]{0:T(512)}, f32[512]{0:T(512)S(1)}, u32[]{:S(2)}, u32[]{:S(2)}) %collective-permute-start.2) | collective-permute-done | bytes 2080 | tf_op jit(solution)/shard_map/ppermute | solution.py:281
  37.5 0.7 add.26
  38.2 0.3 collective-permute-start.3
  38.5 3.2 %collective-permute-done.3 = f32[512]{0:T(512)S(1)} collective-permute-done((f32[512]{0:T(512)S(1)}, f32[512]{0:T(512)S(1)}, u32[]{:S(2)}, u32[]{:S(2)}) %collective-permute-start.3) | collective-permute-done | bytes 2080 | tf_op jit(solution)/shard_map/ppermute | solution.py:281
  41.8 2.2 %collective-permute-start.4 = (f32[512]{0:T(512)S(1)}, f32[512]{0:T(512)S(1)}, u32[]{:S(2)}, u32[]{:S(2)}) collective-permute-start(f32[512]{0:T(512)S(1)} %add.27), channel_id=1, source_target_pairs={{0,6},{1,7},{2,4},{3,5},{4,2},{5,3},{6,0},{7,1},{8,14},{9,15},{10,... | collective-permute-start | bytes 6152 | tf_op jit(solution)/shard_map/ppermute | solution.py:281
  44.0 2.6 %collective-permute-done.4 = f32[512]{0:T(512)S(1)} collective-permute-done((f32[512]{0:T(512)S(1)}, f32[512]{0:T(512)S(1)}, u32[]{:S(2)}, u32[]{:S(2)}) %collective-permute-start.4) | collective-permute-done | bytes 2080 | tf_op jit(solution)/shard_map/ppermute | solution.py:281
  46.6 1.9 %collective-permute-start.5 = (f32[512]{0:T(512)S(1)}, f32[512]{0:T(512)S(1)}, u32[]{:S(2)}, u32[]{:S(2)}) collective-permute-start(f32[512]{0:T(512)S(1)} %add.28), channel_id=1, source_target_pairs={{0,64},{1,65},{2,66},{3,67},{4,68},{5,69},{6,70},{7,71},{8,72},{9,... | collective-permute-start | bytes 6152 | tf_op jit(solution)/shard_map/ppermute | solution.py:281
  48.5 1.7 %collective-permute-done.5 = f32[512]{0:T(512)S(1)} collective-permute-done((f32[512]{0:T(512)S(1)}, f32[512]{0:T(512)S(1)}, u32[]{:S(2)}, u32[]{:S(2)}) %collective-permute-start.5) | collective-permute-done | bytes 2080 | tf_op jit(solution)/shard_map/ppermute | solution.py:281
  50.2 10.0 %collective-permute-start.6 = (f32[512]{0:T(512)S(1)}, f32[512]{0:T(512)S(1)}, u32[]{:S(2)}, u32[]{:S(2)}) collective-permute-start(f32[512]{0:T(512)S(1)} %add.29), channel_id=1, source_target_pairs={{0,72},{1,73},{2,74},{3,75},{4,76},{5,77},{6,78},{7,79},{8,64},{9,... | collective-permute-start | bytes 6152 | tf_op jit(solution)/shard_map/ppermute | solution.py:281
  60.2 1.6 %collective-permute-done.6 = f32[512]{0:T(512)S(1)} collective-permute-done((f32[512]{0:T(512)S(1)}, f32[512]{0:T(512)S(1)}, u32[]{:S(2)}, u32[]{:S(2)}) %collective-permute-start.6) | collective-permute-done | bytes 2080 | tf_op jit(solution)/shard_map/ppermute | solution.py:281
  61.7 1.6 %collective-permute-start.7 = (f32[512]{0:T(512)S(1)}, f32[512]{0:T(512)S(1)}, u32[]{:S(2)}, u32[]{:S(2)}) collective-permute-start(f32[512]{0:T(512)S(1)} %add.30), channel_id=1, source_target_pairs={{0,16},{1,17},{2,18},{3,19},{4,20},{5,21},{6,22},{7,23},{8,24},{9,... | collective-permute-start | bytes 6152 | tf_op jit(solution)/shard_map/ppermute | solution.py:281
  63.3 2.0 %collective-permute-done.7 = f32[512]{0:T(512)S(1)} collective-permute-done((f32[512]{0:T(512)S(1)}, f32[512]{0:T(512)S(1)}, u32[]{:S(2)}, u32[]{:S(2)}) %collective-permute-start.7) | collective-permute-done | bytes 2080 | tf_op jit(solution)/shard_map/ppermute | solution.py:281
  65.3 3.0 %collective-permute-start.8 = (f32[512]{0:T(512)S(1)}, f32[512]{0:T(512)S(1)}, u32[]{:S(2)}, u32[]{:S(2)}) collective-permute-start(f32[512]{0:T(512)S(1)} %add.31), channel_id=1, source_target_pairs={{0,48},{1,49},{2,50},{3,51},{4,52},{5,53},{6,54},{7,55},{8,56},{9,... | collective-permute-start | bytes 6152 | tf_op jit(solution)/shard_map/ppermute | solution.py:281
  68.4 1.8 %collective-permute-done.8 = f32[512]{0:T(512)S(1)} collective-permute-done((f32[512]{0:T(512)S(1)}, f32[512]{0:T(512)S(1)}, u32[]{:S(2)}, u32[]{:S(2)}) %collective-permute-start.8) | collective-permute-done | bytes 2080 | tf_op jit(solution)/shard_map/ppermute | solution.py:281
  70.1 0.6 add.32
  (5 shorter events, 0.0 us)
Async XLA Ops:
  0.0 16.3 %collective-permute-start.1 = (bf16[1024,512]{1,0:T(8,128)(2,1)}, bf16[1024,512]{1,0:T(8,128)(2,1)S(1)}, u32[]{:S(2)}, u32[]{:S(2)}) collective-permute-start(bf16[1024,512]{1,0:T(8,128)(2,1)} %orb_ref.1), channel_id=1, source_target_pairs={{0,1},{1,0},{2,3},{3,2},{4,5},{5,4},{6,7},{7,6},{8,9},{9,8},{10,11... | collective-permute-start | bytes 3145736 | tf_op jit(solution)/shard_map/ppermute | solution.py:288
  0.0 24.2 %collective-permute-start = (bf16[1024,512]{1,0:T(8,128)(2,1)}, bf16[1024,512]{1,0:T(8,128)(2,1)S(1)}, u32[]{:S(2)}, u32[]{:S(2)}) collective-permute-start(bf16[1024,512]{1,0:T(8,128)(2,1)} %orb_ref.1), channel_id=1, source_target_pairs={{1,2},{2,1},{3,4},{4,3},{5,6},{6,5},{7,72},{72,7},{9,10},{10,9},{1... | collective-permute-start | bytes 3145736 | tf_op jit(solution)/shard_map/ppermute | solution.py:287
  16.3 1.0 %copy-start.1 = (bf16[1024,512]{1,0:T(8,128)(2,1)}, bf16[1024,512]{1,0:T(8,128)(2,1)S(1)}, u32[]{:S(2)}) copy-start(bf16[1024,512]{1,0:T(8,128)(2,1)S(1)} %collective-permute-done.1.orb_ref) | copy-start | bytes 3145732
  24.2 1.0 %copy-start = (bf16[1024,512]{1,0:T(8,128)(2,1)}, bf16[1024,512]{1,0:T(8,128)(2,1)S(1)}, u32[]{:S(2)}) copy-start(bf16[1024,512]{1,0:T(8,128)(2,1)S(1)} %collective-permute-done.orb_ref) | copy-start | bytes 3145732
  32.1 5.4 %collective-permute-start.2 = (f32[512]{0:T(512)}, f32[512]{0:T(512)S(1)}, u32[]{:S(2)}, u32[]{:S(2)}) collective-permute-start(f32[512]{0:T(512)} %bitcast.7), channel_id=1, source_target_pairs={{0,1},{1,0},{2,3},{3,2},{4,5},{5,4},{6,7},{7,6},{8,9},{9,8},{10,11... | collective-permute-start | bytes 6152 | tf_op jit(solution)/shard_map/ppermute | solution.py:281
  38.2 3.6 %collective-permute-start.3 = (f32[512]{0:T(512)S(1)}, f32[512]{0:T(512)S(1)}, u32[]{:S(2)}, u32[]{:S(2)}) collective-permute-start(f32[512]{0:T(512)S(1)} %add.26), channel_id=1, source_target_pairs={{0,2},{1,3},{2,0},{3,1},{4,6},{5,7},{6,4},{7,5},{8,10},{9,11},{10,... | collective-permute-start | bytes 6152 | tf_op jit(solution)/shard_map/ppermute | solution.py:281
  41.8 4.8 %collective-permute-start.4 = (f32[512]{0:T(512)S(1)}, f32[512]{0:T(512)S(1)}, u32[]{:S(2)}, u32[]{:S(2)}) collective-permute-start(f32[512]{0:T(512)S(1)} %add.27), channel_id=1, source_target_pairs={{0,6},{1,7},{2,4},{3,5},{4,2},{5,3},{6,0},{7,1},{8,14},{9,15},{10,... | collective-permute-start | bytes 6152 | tf_op jit(solution)/shard_map/ppermute | solution.py:281
  46.6 3.6 %collective-permute-start.5 = (f32[512]{0:T(512)S(1)}, f32[512]{0:T(512)S(1)}, u32[]{:S(2)}, u32[]{:S(2)}) collective-permute-start(f32[512]{0:T(512)S(1)} %add.28), channel_id=1, source_target_pairs={{0,64},{1,65},{2,66},{3,67},{4,68},{5,69},{6,70},{7,71},{8,72},{9,... | collective-permute-start | bytes 6152 | tf_op jit(solution)/shard_map/ppermute | solution.py:281
  50.2 11.6 %collective-permute-start.6 = (f32[512]{0:T(512)S(1)}, f32[512]{0:T(512)S(1)}, u32[]{:S(2)}, u32[]{:S(2)}) collective-permute-start(f32[512]{0:T(512)S(1)} %add.29), channel_id=1, source_target_pairs={{0,72},{1,73},{2,74},{3,75},{4,76},{5,77},{6,78},{7,79},{8,64},{9,... | collective-permute-start | bytes 6152 | tf_op jit(solution)/shard_map/ppermute | solution.py:281
  61.7 3.6 %collective-permute-start.7 = (f32[512]{0:T(512)S(1)}, f32[512]{0:T(512)S(1)}, u32[]{:S(2)}, u32[]{:S(2)}) collective-permute-start(f32[512]{0:T(512)S(1)} %add.30), channel_id=1, source_target_pairs={{0,16},{1,17},{2,18},{3,19},{4,20},{5,21},{6,22},{7,23},{8,24},{9,... | collective-permute-start | bytes 6152 | tf_op jit(solution)/shard_map/ppermute | solution.py:281
  65.3 4.8 %collective-permute-start.8 = (f32[512]{0:T(512)S(1)}, f32[512]{0:T(512)S(1)}, u32[]{:S(2)}, u32[]{:S(2)}) collective-permute-start(f32[512]{0:T(512)S(1)} %add.31), channel_id=1, source_target_pairs={{0,48},{1,49},{2,50},{3,51},{4,52},{5,53},{6,54},{7,55},{8,56},{9,... | collective-permute-start | bytes 6152 | tf_op jit(solution)/shard_map/ppermute | solution.py:281

commit v2 on v1

v2 whole, which is shorter than its diff:
```python
import jax
import jax.numpy as jnp
from jax import lax
from jax.experimental import pallas as pl
from jax.experimental.pallas import tpu as pltpu
from jax.sharding import PartitionSpec as P

ORBS = 512
TILE = 64
HALF = 32
BAND = 16
BLOCK = 4
SPAN = BLOCK * TILE
BLOCKS = BAND // BLOCK
UNROLL = 4
CHUNK = 64

F32 = jnp.float32
BF16 = jnp.bfloat16


def weight_row(energies, node):
    return energies / (energies * energies + node * node)


def scale_into(scaled, points, energies_ref, nodes_ref):
    for f in range(2):
        weight = weight_row(energies_ref[...], nodes_ref[f])
        scaled[f] = (points[...].astype(F32) * weight).astype(BF16)


def block_terms(rows, cols_scaled, cols, w_of, ratio):
    dims = (((1,), (1,)), ((), ()))
    g0 = lax.dot_general(rows, cols_scaled(0), dims, preferred_element_type=F32)
    g1 = lax.dot_general(rows, cols_scaled(1), dims, preferred_element_type=F32)
    product = g0 * w_of(0).astype(F32) + ratio * (g1 * w_of(1).astype(F32))
    image = jnp.dot(product.astype(BF16), cols(), preferred_element_type=F32)
    return jnp.sum(image * rows.astype(F32), axis=0, keepdims=True)


def own_kernel(
    count_ref,
    rows_ref,
    cols_ref,
    nodes_ref,
    weights_ref,
    orb_ref,
    energies_ref,
    screened_ref,
    sigma_ref,
    perm,
    halo,
    points,
    raw,
    dense,
    own_w,
    scaled,
    wide,
    raw_sem,
    orb_sem,
):
    slots = screened_ref.shape[0]
    chunks = slots // CHUNK
    count = count_ref[0]
    first = (lax.axis_index("pts") - 1) * BAND

    def fetch(k):
        part = pl.ds(k * CHUNK, CHUNK)
        return pltpu.make_async_copy(screened_ref.at[part], raw.at[part], raw_sem.at[k])

    bring = pltpu.make_async_copy(orb_ref, points, orb_sem)
    bring.start()
    for k in range(chunks):

        @pl.when(k * CHUNK < count)
        def _():
            fetch(k).start()

    for b in range(BLOCKS):

        def clear(r, carry):
            for c in range(b * BLOCK, b * BLOCK + 2 * BAND + BLOCK):
                dense[r, c] = jnp.zeros(dense.shape[2:], F32)
            return carry

        lax.fori_loop(b * BLOCK, (b + 1) * BLOCK, clear, 0)
    bring.wait()

    for q in range(ORBS // 128):
        lanes = pl.ds(q * 128, 128)
        wide[q] = points[:, lanes].astype(F32)
        for b in range(BLOCKS):
            for h in range(2):
                perm[pl.ds(b * SPAN + h * SPAN // 2, SPAN // 2), lanes] = wide[
                    q, pl.ds(b * SPAN + h, SPAN // 2, stride=2), :
                ].astype(BF16)
    scale_into(scaled, points, energies_ref, nodes_ref)

    def place(s):
        return rows_ref[s], cols_ref[s] - first

    def scatter(s, carry):
        r, c = place(s)
        dense[r, c] = dense[r, c] + raw[s].astype(F32)
        return carry

    for k in range(chunks):

        @pl.when(k * CHUNK < count)
        def _():
            fetch(k).wait()
            here = jnp.minimum(count - k * CHUNK, CHUNK)

            def several(i, carry):
                for d in range(UNROLL):
                    scatter(k * CHUNK + i * UNROLL + d, 0)
                return carry

            whole = here // UNROLL
            lax.fori_loop(0, whole, several, 0)
            lax.fori_loop(k * CHUNK + whole * UNROLL, k * CHUNK + here, scatter, 0)

    low = lax.broadcasted_iota(jnp.int32, (SPAN // 2, 2 * TILE), 1) < TILE

    def arrange(side, f, b, pair):
        to_b = BLOCKS - 1 - b if side == 0 else b
        to_pair = (BLOCKS - 1 - pair // 2) * 2 + pair % 2 if side == 0 else pair
        parts = []
        for d in range(2):
            c = side * BAND + 2 * pair + d
            parts.append(dense[pl.ds(b * BLOCK, BLOCK), c, f, :].reshape(SPAN // 2, 2 * TILE))
        v0, v1 = parts
        even = jnp.where(low, v0, pltpu.roll(v1, TILE, 1))
        odd = jnp.where(low, pltpu.roll(v0, TILE, 1), v1)
        lanes = pl.ds(to_pair * 2 * TILE, 2 * TILE)
        to = own_w.at[f] if side == 1 else halo.at[side // 2, f]
        to[pl.ds(to_b * SPAN, SPAN // 2), lanes] = even.astype(BF16)
        to[pl.ds(to_b * SPAN + SPAN // 2, SPAN // 2), lanes] = odd.astype(BF16)

    def arrange_block(side, b, c):
        for f in range(2):
            for pair in range(2 * c, 2 * c + 2):
                arrange(side, f, b, pair)

    for b in range(BLOCKS):
        for c in range(BLOCKS):
            if c >= b:
                arrange_block(0, b, c)
            if c <= b:
                arrange_block(2, b, c)
    ratio = weights_ref[1] / weights_ref[0]
    total = jnp.zeros((1, ORBS), F32)
    for b in range(BLOCKS):
        for c in range(BLOCKS):
            arrange_block(1, b, c)
        total += block_terms(
            perm[pl.ds(b * SPAN, SPAN), :],
            lambda f: scaled[f],
            lambda: points[...],
            lambda f: own_w[f, pl.ds(b * SPAN, SPAN), :],
            ratio,
        )
    sigma_ref[...] = -weights_ref[0] * total


def own_part(count, rows, cols, nodes, weights, orbitals, energies, screened):
    points = orbitals.shape[0]
    smem = pl.BlockSpec(memory_space=pltpu.SMEM)
    vmem = pl.BlockSpec(memory_space=pltpu.VMEM)
    hbm = pl.BlockSpec(memory_space=pl.ANY)
    return pl.pallas_call(
        own_kernel,
        out_shape=(
            pltpu.VMEM((1, ORBS), F32),
            pltpu.VMEM((points, ORBS), BF16),
            pltpu.VMEM((2, 2, points, points), BF16),
        ),
        in_specs=[smem] * 5 + [hbm, vmem, hbm],
        out_specs=(vmem, vmem, vmem),
        scratch_shapes=[
            pltpu.VMEM((points, ORBS), BF16),
            pltpu.VMEM(screened.shape, BF16),
            pltpu.VMEM((BAND, 3 * BAND, 2, TILE * TILE), F32),
            pltpu.VMEM((2, points, points), BF16),
            pltpu.VMEM((2, points, ORBS), BF16),
            pltpu.VMEM((ORBS // 128, points, 128), F32),
            pltpu.SemaphoreType.DMA((screened.shape[0] // CHUNK,)),
            pltpu.SemaphoreType.DMA,
        ],
        compiler_params=pltpu.CompilerParams(vmem_limit_bytes=46 << 20),
    )(count, rows, cols, nodes, weights, orbitals, energies, screened)


def halo_kernel(
    side_ref,
    nodes_ref,
    weights_ref,
    energies_ref,
    sigma_in,
    perm_ref,
    orb_ref,
    halo_ref,
    sigma_ref,
    points,
    scaled,
):
    side = side_ref[0]
    ratio = weights_ref[1] / weights_ref[0]
    total = jnp.zeros((1, ORBS), F32)
    for u in range(BLOCKS):
        block = (1 - side) * (BLOCKS - 1 - u) + side * u
        from_rows = pl.ds(pl.multiple_of(block * SPAN, SPAN), SPAN)
        rows = pl.ds(u * SPAN, SPAN)
        cols = pl.ds(0, (u + 1) * SPAN)
        points[rows, :] = orb_ref[from_rows, :]
        for f in range(2):
            weight = weight_row(energies_ref[...], nodes_ref[f])
            scaled[f, rows] = (points[rows, :].astype(F32) * weight).astype(BF16)
        total += block_terms(
            perm_ref[from_rows, :],
            lambda f: scaled[f, cols, :],
            lambda: points[cols, :],
            lambda f: halo_ref[side, f, rows, cols],
            ratio,
        )
    sigma_ref[...] = sigma_in[...] - weights_ref[0] * total


def halo_part(side, nodes, weights, perm, orbitals, energies, sigma, halo):
    points = orbitals.shape[0]
    smem = pl.BlockSpec(memory_space=pltpu.SMEM)
    vmem = pl.BlockSpec(memory_space=pltpu.VMEM)
    return pl.pallas_call(
        halo_kernel,
        out_shape=pltpu.VMEM((1, ORBS), F32),
        in_specs=[smem] * 3 + [vmem] * 5,
        out_specs=vmem,
        scratch_shapes=[
            pltpu.VMEM((points, ORBS), BF16),
            pltpu.VMEM((2, points, ORBS), BF16),
        ],
        compiler_params=pltpu.CompilerParams(vmem_limit_bytes=16 << 20),
    )(
        side,
        nodes,
        weights,
        energies,
        pltpu.with_memory_space_constraint(sigma, pltpu.VMEM),
        pltpu.with_memory_space_constraint(perm, pltpu.VMEM),
        pltpu.with_memory_space_constraint(orbitals, pltpu.VMEM),
        pltpu.with_memory_space_constraint(halo, pltpu.VMEM),
    )


AXES = ("freq", "pts")


def device(f, p):
    return f * 16 + p


def inner_pairs():
    return [(device(f, p), device(f, p ^ 1)) for f in range(8) for p in range(16)]


def outer_pairs():
    pairs = []
    for f in range(8):
        for p in range(1, 15, 2):
            to = device(f ^ 4 if p == 7 else f, p + 1)
            pairs += [(device(f, p), to), (to, device(f, p))]
    return pairs


def total_over_devices(x):
    for mask in (1, 2, 6, 64, 72, 16, 48):
        x = x + lax.ppermute(x, AXES, [(i, i ^ mask) for i in range(128)])
    return x


def body(orbitals, energies, freq_nodes, weights_q, screened, tile_rows, tile_cols, tile_count):
    position = lax.axis_index("pts")
    outer = lax.ppermute(orbitals, AXES, outer_pairs())
    inner = lax.ppermute(orbitals, AXES, inner_pairs())
    energies = energies[None, :]
    sigma, perm, halo = own_part(
        tile_count, tile_rows, tile_cols, freq_nodes, weights_q, orbitals, energies, screened
    )
    odd = (position % 2).astype(jnp.int32)
    for side, points in ((1 - odd, inner), (odd, outer)):
        sigma = halo_part(
            side[None], freq_nodes, weights_q, perm, points, energies, sigma, halo
        )
    return total_over_devices(sigma[0])


def solution(mesh):
    placed = (
        P("pts", None),
        P(),
        P("freq"),
        P("freq"),
        P("pts", "freq", None),
        P("pts"),
        P("pts"),
        P("pts"),
    )
    return jax.shard_map(body, mesh=mesh, in_specs=placed, out_specs=P(), check_vma=False)
```

time: 70.6 us -> 52.7 us (0.75)
  Pallas kernels: 28.8 us -> 17.5 us
  starting transfers between devices: 24.2 us -> 21.4 us
  waiting for transfers between devices: 13.9 us -> 11.9 us
  local copies, waits for them, and re-layouts: 1.89 us -> 0.01 us
    pallas_call x3, Pallas kernels: 28.8 us -> 17.5 us  [the longest x1 11 us: own_part(): pl.pallas_call(own_kernel, out_shape=(pltpu.VMEM((1, ORBS), F32), pltpu.V...]
    ppermute x7, starting transfers between devices: 23.4 us -> 20.6 us  [total_over_devices(): x = x + lax.ppermute(x, AXES, [(i, i ^ mask) for i in range(128)])]
    ppermute x7, waiting for transfers between devices: 13.9 us -> 11.9 us  [total_over_devices(): x = x + lax.ppermute(x, AXES, [(i, i ^ mask) for i in range(128)])]
    unnamed x4 -> x6, local copies, waits for them, and re-layouts: 1.89 us -> 0.01 us
  transfers between devices with their start and end apart: 9 -> 9, of which waited for: 7 -> 7; matrix products, arithmetic and copies ran while one was open for 0% -> 0% of each run, Pallas kernels for 31% -> 27%
where the time goes in v2:
time: 52.7 us; the launch traced here: 52.2 us
  starting transfers between devices  21.4 us (41%)
  Pallas kernels  17.5 us (33%)
  waiting for transfers between devices  11.9 us (23%)
  between operations  0.74 us (1%)
  other arithmetic  0.6 us (1%)
    ppermute x7, starting transfers between devices, total_over_devices(): x = x + lax.ppermute(x, AXES, [(i, i ^ mask) for i in range(128)])  20.6 us
    ppermute x7, waiting for transfers between devices, total_over_devices(): x = x + lax.ppermute(x, AXES, [(i, i ^ mask) for i in range(128)])  11.9 us
    pallas_call x1, Pallas kernels, own_part(): pl.pallas_call(own_kernel, out_shape=(pltpu.VMEM((1, ORBS), F32), pltpu.V...  11 us
    pallas_call x2, Pallas kernels, halo_part(): pl.pallas_call(halo_kernel, out_shape=pltpu.VMEM((1, ORBS), F32), in_spec...  6.5 us
  transfers between devices with their start and end apart: 9, of which 7 were waited for; matrix products, arithmetic and copies ran while one was open for 0% of the time, Pallas kernels for 27%

profile of v2, /device:TPU:0, one launch (start us, length us, event | category | flops | bytes accessed | tf_op | source)
XLA Modules:
  0.0 52.2 jit_solution(16744327818003949113)
XLA Ops:
  0.0 0.0 copy-start
  0.0 0.0 copy-start.1
  0.0 0.0 copy-start.2
  0.0 0.0 collective-permute-start
  0.0 0.9 %collective-permute-start.1 = (bf16[1024,512]{1,0:T(8,128)(2,1)}, bf16[1024,512]{1,0:T(8,128)(2,1)S(1)}, u32[]{:S(2)}, u32[]{:S(2)}) collective-permute-start(bf16[1024,512]{1,0:T(8,128)(2,1)} %orb_ref.1), channel_id=1, source_target_pairs={{1,2},{2,1},{3,4},{4,3},{5,6},{6,5},{7,72},{72,7},{9,10},{10,9},{1... | collective-permute-start | bytes 3145736 | tf_op jit(solution)/shard_map/ppermute | solution.py:283
  1.5 11.0 %shard_map.82 = (f32[1,512]{1,0:T(1,128)S(1)}, bf16[1024,512]{1,0:T(8,128)(2,1)S(1)}, bf16[2,2,1024,1024]{3,2,1,0:T(8,128)(2,1)S(1)}) custom-call(s32[1]{0:T(128)S(6)} %copy.9.count_ref, s32[512]{0:T(512)} %rows_ref.1, s32[512]{0:T(512)} %cols_ref.1, f32[2]{0:T(128)} %nodes_ref.5, f32[2]{0:T(128)} %weights_ref.5, bf16[1024,512]{1,0:T(8,128)(2,1)} %orb_ref.1, ...), custom_call_target="tpu_custom_call" | custom-call | tf_op jit(solution)/shard_map/pallas_call | solution.py:171
  12.5 0.0 collective-permute-done.orb_ref
  12.5 0.0 copy-done
  12.5 0.0 copy-done.1
  12.6 0.0 copy-done.2
  12.6 3.3 %shard_map.83.sigma_in = f32[1,512]{1,0:T(1,128)S(1)} custom-call(s32[1]{0:T(128)} %bitcast.2.side_ref, f32[2]{0:T(128)S(1)} %copy-done.1, f32[2]{0:T(128)S(1)} %copy-done.2, f32[1,512]{1,0:T(1,128)S(1)} %bitcast.5, f32[1,512]{1,0:T(1,128)S(1)} %get-tuple-element.8.sigma_in, bf16[1024,512]{1,0:T(8,128)(2,1)S(1)} %get-tuple-element.9.perm_ref, ...), custom_call_target="tpu_custom_call" | custom-call | tf_op jit(solution)/shard_map/pallas_call | solution.py:233
  15.8 0.0 collective-permute-done.1.orb_ref
  15.8 3.2 %shard_map.84 = f32[1,512]{1,0:T(1,128)S(1)} custom-call(s32[1]{0:T(128)} %bitcast.side_ref, f32[2]{0:T(128)S(1)} %copy-done.1, f32[2]{0:T(128)S(1)} %copy-done.2, f32[1,512]{1,0:T(1,128)S(1)} %bitcast.6, f32[1,512]{1,0:T(1,128)S(1)} %shard_map.83.sigma_in, bf16[1024,512]{1,0:T(8,128)(2,1)S(1)} %get-tuple-element.9.perm_ref, ...), custom_call_target="tpu_custom_call" | custom-call | tf_op jit(solution)/shard_map/pallas_call | solution.py:233
  19.1 2.7 %collective-permute-start.2 = (f32[512]{0:T(512)S(1)}, f32[512]{0:T(512)S(1)}, u32[]{:S(2)}, u32[]{:S(2)}) collective-permute-start(f32[512]{0:T(512)S(1)} %bitcast.7), channel_id=1, source_target_pairs={{0,1},{1,0},{2,3},{3,2},{4,5},{5,4},{6,7},{7,6},{8,9},{9,8},{10,11... | collective-permute-start | bytes 6152 | tf_op jit(solution)/shard_map/ppermute | solution.py:277
  21.7 0.8 %collective-permute-done.2 = f32[512]{0:T(512)S(1)} collective-permute-done((f32[512]{0:T(512)S(1)}, f32[512]{0:T(512)S(1)}, u32[]{:S(2)}, u32[]{:S(2)}) %collective-permute-start.2) | collective-permute-done | bytes 2080 | tf_op jit(solution)/shard_map/ppermute | solution.py:277
  22.6 2.5 %collective-permute-start.3 = (f32[512]{0:T(512)S(1)}, f32[512]{0:T(512)S(1)}, u32[]{:S(2)}, u32[]{:S(2)}) collective-permute-start(f32[512]{0:T(512)S(1)} %add.26), channel_id=1, source_target_pairs={{0,2},{1,3},{2,0},{3,1},{4,6},{5,7},{6,4},{7,5},{8,10},{9,11},{10,... | collective-permute-start | bytes 6152 | tf_op jit(solution)/shard_map/ppermute | solution.py:277
  25.1 1.6 %collective-permute-done.3 = f32[512]{0:T(512)S(1)} collective-permute-done((f32[512]{0:T(512)S(1)}, f32[512]{0:T(512)S(1)}, u32[]{:S(2)}, u32[]{:S(2)}) %collective-permute-start.3) | collective-permute-done | bytes 2080 | tf_op jit(solution)/shard_map/ppermute | solution.py:277
  26.6 4.2 %collective-permute-start.4 = (f32[512]{0:T(512)S(1)}, f32[512]{0:T(512)S(1)}, u32[]{:S(2)}, u32[]{:S(2)}) collective-permute-start(f32[512]{0:T(512)S(1)} %add.27), channel_id=1, source_target_pairs={{0,6},{1,7},{2,4},{3,5},{4,2},{5,3},{6,0},{7,1},{8,14},{9,15},{10,... | collective-permute-start | bytes 6152 | tf_op jit(solution)/shard_map/ppermute | solution.py:277
  30.8 1.6 %collective-permute-done.4 = f32[512]{0:T(512)S(1)} collective-permute-done((f32[512]{0:T(512)S(1)}, f32[512]{0:T(512)S(1)}, u32[]{:S(2)}, u32[]{:S(2)}) %collective-permute-start.4) | collective-permute-done | bytes 2080 | tf_op jit(solution)/shard_map/ppermute | solution.py:277
  32.4 1.0 %collective-permute-start.5 = (f32[512]{0:T(512)S(1)}, f32[512]{0:T(512)S(1)}, u32[]{:S(2)}, u32[]{:S(2)}) collective-permute-start(f32[512]{0:T(512)S(1)} %add.28), channel_id=1, source_target_pairs={{0,64},{1,65},{2,66},{3,67},{4,68},{5,69},{6,70},{7,71},{8,72},{9,... | collective-permute-start | bytes 6152 | tf_op jit(solution)/shard_map/ppermute | solution.py:277
  33.3 2.6 %collective-permute-done.5 = f32[512]{0:T(512)S(1)} collective-permute-done((f32[512]{0:T(512)S(1)}, f32[512]{0:T(512)S(1)}, u32[]{:S(2)}, u32[]{:S(2)}) %collective-permute-start.5) | collective-permute-done | bytes 2080 | tf_op jit(solution)/shard_map/ppermute | solution.py:277
  36.0 5.7 %collective-permute-start.6 = (f32[512]{0:T(512)S(1)}, f32[512]{0:T(512)S(1)}, u32[]{:S(2)}, u32[]{:S(2)}) collective-permute-start(f32[512]{0:T(512)S(1)} %add.29), channel_id=1, source_target_pairs={{0,72},{1,73},{2,74},{3,75},{4,76},{5,77},{6,78},{7,79},{8,64},{9,... | collective-permute-start | bytes 6152 | tf_op jit(solution)/shard_map/ppermute | solution.py:277
  41.7 1.6 %collective-permute-done.6 = f32[512]{0:T(512)S(1)} collective-permute-done((f32[512]{0:T(512)S(1)}, f32[512]{0:T(512)S(1)}, u32[]{:S(2)}, u32[]{:S(2)}) %collective-permute-start.6) | collective-permute-done | bytes 2080 | tf_op jit(solution)/shard_map/ppermute | solution.py:277
  43.2 1.6 %collective-permute-start.7 = (f32[512]{0:T(512)S(1)}, f32[512]{0:T(512)S(1)}, u32[]{:S(2)}, u32[]{:S(2)}) collective-permute-start(f32[512]{0:T(512)S(1)} %add.30), channel_id=1, source_target_pairs={{0,16},{1,17},{2,18},{3,19},{4,20},{5,21},{6,22},{7,23},{8,24},{9,... | collective-permute-start | bytes 6152 | tf_op jit(solution)/shard_map/ppermute | solution.py:277
  44.8 2.0 %collective-permute-done.7 = f32[512]{0:T(512)S(1)} collective-permute-done((f32[512]{0:T(512)S(1)}, f32[512]{0:T(512)S(1)}, u32[]{:S(2)}, u32[]{:S(2)}) %collective-permute-start.7) | collective-permute-done | bytes 2080 | tf_op jit(solution)/shard_map/ppermute | solution.py:277
  46.8 3.0 %collective-permute-start.8 = (f32[512]{0:T(512)S(1)}, f32[512]{0:T(512)S(1)}, u32[]{:S(2)}, u32[]{:S(2)}) collective-permute-start(f32[512]{0:T(512)S(1)} %add.31), channel_id=1, source_target_pairs={{0,48},{1,49},{2,50},{3,51},{4,52},{5,53},{6,54},{7,55},{8,56},{9,... | collective-permute-start | bytes 6152 | tf_op jit(solution)/shard_map/ppermute | solution.py:277
  49.8 1.8 %collective-permute-done.8 = f32[512]{0:T(512)S(1)} collective-permute-done((f32[512]{0:T(512)S(1)}, f32[512]{0:T(512)S(1)}, u32[]{:S(2)}, u32[]{:S(2)}) %collective-permute-start.8) | collective-permute-done | bytes 2080 | tf_op jit(solution)/shard_map/ppermute | solution.py:277
  51.6 0.6 %add.32 = f32[512]{0:T(512)} add(f32[512]{0:T(512)S(1)} %add.31, f32[512]{0:T(512)S(1)} %collective-permute-done.8) | non-fusion elementwise | flops 512 | bytes 6144 | tf_op jit(solution)/shard_map/add | solution.py:277
  (6 shorter events, 0.0 us)
Async XLA Ops:
  0.0 12.5 %copy-start = (f32[512]{0:T(512)S(1)}, f32[512]{0:T(512)}, u32[]{:S(2)}) copy-start(f32[512]{0:T(512)} %param.9) | copy-start | bytes 6148
  0.0 12.5 %copy-start.1 = (f32[2]{0:T(128)S(1)}, f32[2]{0:T(128)}, u32[]{:S(2)}) copy-start(f32[2]{0:T(128)} %nodes_ref.5) | copy-start | bytes 28
  0.0 12.5 %copy-start.2 = (f32[2]{0:T(128)S(1)}, f32[2]{0:T(128)}, u32[]{:S(2)}) copy-start(f32[2]{0:T(128)} %weights_ref.5) | copy-start | bytes 28
  0.0 12.5 %collective-permute-start = (bf16[1024,512]{1,0:T(8,128)(2,1)}, bf16[1024,512]{1,0:T(8,128)(2,1)S(1)}, u32[]{:S(2)}, u32[]{:S(2)}) collective-permute-start(bf16[1024,512]{1,0:T(8,128)(2,1)} %orb_ref.1), channel_id=1, source_target_pairs={{0,1},{1,0},{2,3},{3,2},{4,5},{5,4},{6,7},{7,6},{8,9},{9,8},{10,11... | collective-permute-start | bytes 3145736 | tf_op jit(solution)/shard_map/ppermute | solution.py:284
  0.0 15.8 %collective-permute-start.1 = (bf16[1024,512]{1,0:T(8,128)(2,1)}, bf16[1024,512]{1,0:T(8,128)(2,1)S(1)}, u32[]{:S(2)}, u32[]{:S(2)}) collective-permute-start(bf16[1024,512]{1,0:T(8,128)(2,1)} %orb_ref.1), channel_id=1, source_target_pairs={{1,2},{2,1},{3,4},{4,3},{5,6},{6,5},{7,72},{72,7},{9,10},{10,9},{1... | collective-permute-start | bytes 3145736 | tf_op jit(solution)/shard_map/ppermute | solution.py:283
  19.1 3.5 %collective-permute-start.2 = (f32[512]{0:T(512)S(1)}, f32[512]{0:T(512)S(1)}, u32[]{:S(2)}, u32[]{:S(2)}) collective-permute-start(f32[512]{0:T(512)S(1)} %bitcast.7), channel_id=1, source_target_pairs={{0,1},{1,0},{2,3},{3,2},{4,5},{5,4},{6,7},{7,6},{8,9},{9,8},{10,11... | collective-permute-start | bytes 6152 | tf_op jit(solution)/shard_map/ppermute | solution.py:277
  22.6 4.1 %collective-permute-start.3 = (f32[512]{0:T(512)S(1)}, f32[512]{0:T(512)S(1)}, u32[]{:S(2)}, u32[]{:S(2)}) collective-permute-start(f32[512]{0:T(512)S(1)} %add.26), channel_id=1, source_target_pairs={{0,2},{1,3},{2,0},{3,1},{4,6},{5,7},{6,4},{7,5},{8,10},{9,11},{10,... | collective-permute-start | bytes 6152 | tf_op jit(solution)/shard_map/ppermute | solution.py:277
  26.6 5.8 %collective-permute-start.4 = (f32[512]{0:T(512)S(1)}, f32[512]{0:T(512)S(1)}, u32[]{:S(2)}, u32[]{:S(2)}) collective-permute-start(f32[512]{0:T(512)S(1)} %add.27), channel_id=1, source_target_pairs={{0,6},{1,7},{2,4},{3,5},{4,2},{5,3},{6,0},{7,1},{8,14},{9,15},{10,... | collective-permute-start | bytes 6152 | tf_op jit(solution)/shard_map/ppermute | solution.py:277
  32.4 3.6 %collective-permute-start.5 = (f32[512]{0:T(512)S(1)}, f32[512]{0:T(512)S(1)}, u32[]{:S(2)}, u32[]{:S(2)}) collective-permute-start(f32[512]{0:T(512)S(1)} %add.28), channel_id=1, source_target_pairs={{0,64},{1,65},{2,66},{3,67},{4,68},{5,69},{6,70},{7,71},{8,72},{9,... | collective-permute-start | bytes 6152 | tf_op jit(solution)/shard_map/ppermute | solution.py:277
  36.0 7.2 %collective-permute-start.6 = (f32[512]{0:T(512)S(1)}, f32[512]{0:T(512)S(1)}, u32[]{:S(2)}, u32[]{:S(2)}) collective-permute-start(f32[512]{0:T(512)S(1)} %add.29), channel_id=1, source_target_pairs={{0,72},{1,73},{2,74},{3,75},{4,76},{5,77},{6,78},{7,79},{8,64},{9,... | collective-permute-start | bytes 6152 | tf_op jit(solution)/shard_map/ppermute | solution.py:277
  43.2 3.6 %collective-permute-start.7 = (f32[512]{0:T(512)S(1)}, f32[512]{0:T(512)S(1)}, u32[]{:S(2)}, u32[]{:S(2)}) collective-permute-start(f32[512]{0:T(512)S(1)} %add.30), channel_id=1, source_target_pairs={{0,16},{1,17},{2,18},{3,19},{4,20},{5,21},{6,22},{7,23},{8,24},{9,... | collective-permute-start | bytes 6152 | tf_op jit(solution)/shard_map/ppermute | solution.py:277
  46.8 4.8 %collective-permute-start.8 = (f32[512]{0:T(512)S(1)}, f32[512]{0:T(512)S(1)}, u32[]{:S(2)}, u32[]{:S(2)}) collective-permute-start(f32[512]{0:T(512)S(1)} %add.31), channel_id=1, source_target_pairs={{0,48},{1,49},{2,50},{3,51},{4,52},{5,53},{6,54},{7,55},{8,56},{9,... | collective-permute-start | bytes 6152 | tf_op jit(solution)/shard_map/ppermute | solution.py:277

commit v3 on v2

--- a/solution.py
+++ b/solution.py
@@ -21,12 +21,6 @@
 
 def weight_row(energies, node):
     return energies / (energies * energies + node * node)
-
-
-def scale_into(scaled, points, energies_ref, nodes_ref):
-    for f in range(2):
-        weight = weight_row(energies_ref[...], nodes_ref[f])
-        scaled[f] = (points[...].astype(F32) * weight).astype(BF16)
 
 
 def block_terms(rows, cols_scaled, cols, w_of, ratio):
@@ -88,13 +82,15 @@
 
     for q in range(ORBS // 128):
         lanes = pl.ds(q * 128, 128)
-        wide[q] = points[:, lanes].astype(F32)
+        values = points[:, lanes].astype(F32)
+        wide[q] = values
+        for f in range(2):
+            weight = weight_row(energies_ref[:, lanes], nodes_ref[f])
+            scaled[f, :, lanes] = (values * weight).astype(BF16)
         for b in range(BLOCKS):
             for h in range(2):
-                perm[pl.ds(b * SPAN + h * SPAN // 2, SPAN // 2), lanes] = wide[
-                    q, pl.ds(b * SPAN + h, SPAN // 2, stride=2), :
-                ].astype(BF16)
-    scale_into(scaled, points, energies_ref, nodes_ref)
+                part = wide[q, pl.ds(b * SPAN + h, SPAN // 2, stride=2), :]
+                perm[pl.ds(b * SPAN + h * SPAN // 2, SPAN // 2), lanes] = part.astype(BF16)
 
     def place(s):
         return rows_ref[s], cols_ref[s] - first
@@ -273,9 +269,9 @@
 
 
 def total_over_devices(x):
-    for mask in (1, 2, 6, 64, 72, 16, 48):
-        x = x + lax.ppermute(x, AXES, [(i, i ^ mask) for i in range(128)])
-    return x
+    count = lax.axis_size(AXES)
+    sent = jnp.broadcast_to(x, (count, ORBS))
+    return jnp.sum(lax.all_to_all(sent, AXES, 0, 0, tiled=True), axis=0)
 
 
 def body(orbitals, energies, freq_nodes, weights_q, screened, tile_rows, tile_cols, tile_count):
@@ -291,7 +287,7 @@
         sigma = halo_part(
             side[None], freq_nodes, weights_q, perm, points, energies, sigma, halo
         )
-    return total_over_devices(sigma[0])
+    return total_over_devices(sigma)
 
 
 def solution(mesh):

time: 52.7 us -> 45.7 us (0.87)
  the two profiles are of different devices: /device:TPU:0 before, /device:TPU:1 now
where the time goes in v3:
time: 45.7 us; the launch traced here: 44.9 us
  blocking collectives  21.5 us (47%)
  Pallas kernels  17.1 us (37%)
  starting transfers between devices  4.6 us (10%)
  other arithmetic  0.79 us (2%)
  between operations  0.74 us (2%)
    all_to_all x1, blocking collectives, total_over_devices(): return jnp.sum(lax.all_to_all(sent, AXES, 0, 0, tiled=True), axis=0)  21.5 us
    pallas_call x1, Pallas kernels, own_part(): pl.pallas_call(own_kernel, out_shape=(pltpu.VMEM((1, ORBS), F32), pltpu.V...  10.6 us
    pallas_call x2, Pallas kernels, halo_part(): pl.pallas_call(halo_kernel, out_shape=pltpu.VMEM((1, ORBS), F32), in_spec...  6.5 us
    ppermute x1, starting transfers between devices, body(): outer = lax.ppermute(orbitals, AXES, outer_pairs())  3.18 us
    ppermute x1, starting transfers between devices, body(): inner = lax.ppermute(orbitals, AXES, inner_pairs())  1.42 us
  transfers between devices with their start and end apart: 2, of which 0 were waited for; matrix products, arithmetic and copies ran while one was open for 0% of the time, Pallas kernels for 31%

profile of v3, /device:TPU:1, one launch (start us, length us, event | category | flops | bytes accessed | tf_op | source)
XLA Modules:
  0.0 44.9 jit_solution(4535133047847402429)
XLA Ops:
  0.0 0.0 copy-start
  0.0 0.0 copy-start.1
  0.0 0.0 copy-start.2
  0.0 1.4 %collective-permute-start = (bf16[1024,512]{1,0:T(8,128)(2,1)}, bf16[1024,512]{1,0:T(8,128)(2,1)S(1)}, u32[]{:S(2)}, u32[]{:S(2)}) collective-permute-start(bf16[1024,512]{1,0:T(8,128)(2,1)} %orb_ref.1), channel_id=1, source_target_pairs={{0,1},{1,0},{2,3},{3,2},{4,5},{5,4},{6,7},{7,6},{8,9},{9,8},{10,11... | collective-permute-start | bytes 3145736 | tf_op jit(solution)/shard_map/ppermute | solution.py:280
  1.4 3.2 %collective-permute-start.1 = (bf16[1024,512]{1,0:T(8,128)(2,1)}, bf16[1024,512]{1,0:T(8,128)(2,1)S(1)}, u32[]{:S(2)}, u32[]{:S(2)}) collective-permute-start(bf16[1024,512]{1,0:T(8,128)(2,1)} %orb_ref.1), channel_id=1, source_target_pairs={{1,2},{2,1},{3,4},{4,3},{5,6},{6,5},{7,72},{72,7},{9,10},{10,9},{1... | collective-permute-start | bytes 3145736 | tf_op jit(solution)/shard_map/ppermute | solution.py:279
  5.3 10.6 %shard_map.82 = (f32[1,512]{1,0:T(1,128)S(1)}, bf16[1024,512]{1,0:T(8,128)(2,1)S(1)}, bf16[2,2,1024,1024]{3,2,1,0:T(8,128)(2,1)S(1)}) custom-call(s32[1]{0:T(128)S(6)} %copy.11.count_ref, s32[512]{0:T(512)} %rows_ref.1, s32[512]{0:T(512)} %cols_ref.1, f32[2]{0:T(128)} %nodes_ref.5, f32[2]{0:T(128)} %weights_ref.5, bf16[1024,512]{1,0:T(8,128)(2,1)} %orb_ref.1, ...), custom_call_target="tpu_custom_call" | custom-call | tf_op jit(solution)/shard_map/pallas_call | solution.py:167
  15.9 0.0 collective-permute-done.orb_ref
  15.9 0.0 copy-done
  15.9 0.0 copy-done.1
  15.9 0.0 copy-done.2
  15.9 3.3 %shard_map.83.sigma_in = f32[1,512]{1,0:T(1,128)S(1)} custom-call(s32[1]{0:T(128)} %bitcast.2.side_ref, f32[2]{0:T(128)S(1)} %copy-done.1, f32[2]{0:T(128)S(1)} %copy-done.2, f32[1,512]{1,0:T(1,128)S(1)} %bitcast.5, f32[1,512]{1,0:T(1,128)S(1)} %get-tuple-element.8.sigma_in, bf16[1024,512]{1,0:T(8,128)(2,1)S(1)} %get-tuple-element.9.perm_ref, ...), custom_call_target="tpu_custom_call" | custom-call | tf_op jit(solution)/shard_map/pallas_call | solution.py:229
  19.2 0.0 collective-permute-done.1.orb_ref
  19.2 3.3 %shard_map.84 = f32[1,512]{1,0:T(1,128)S(1)} custom-call(s32[1]{0:T(128)} %bitcast.side_ref, f32[2]{0:T(128)S(1)} %copy-done.1, f32[2]{0:T(128)S(1)} %copy-done.2, f32[1,512]{1,0:T(1,128)S(1)} %bitcast.6, f32[1,512]{1,0:T(1,128)S(1)} %shard_map.83.sigma_in, bf16[1024,512]{1,0:T(8,128)(2,1)S(1)} %get-tuple-element.9.perm_ref, ...), custom_call_target="tpu_custom_call" | custom-call | tf_op jit(solution)/shard_map/pallas_call | solution.py:229
  22.5 0.1 broadcast_in_dim.17
  22.6 21.5 %all_to_all.6 = f32[128,1,512]{2,1,0:T(1,128)S(1)} all-to-all(f32[128,1,512]{2,1,0:T(1,128)S(1)} %broadcast_in_dim.17), channel_id=1, replica_groups=mesh['freq'=8,'pts'=16] {'freq','pts'}, dimensions={0} | all-to-all | bytes 524288 | tf_op jit(solution)/shard_map/all_to_all | solution.py:274
  44.1 0.8 %reduce_sum.9 = f32[512]{0:T(512)} reduce(f32[128,1,512]{2,1,0:T(1,128)S(1)} %all_to_all.6, f32[]{:T(128)} %constant.19.clone.1), dimensions={0,1}, to_apply=%region_0.1 | reduce | flops 65024 | bytes 264196 | tf_op jit(solution)/shard_map/reduce_sum | solution.py:274
Async XLA Ops:
  0.0 15.9 %copy-start = (f32[512]{0:T(512)S(1)}, f32[512]{0:T(512)}, u32[]{:S(2)}) copy-start(f32[512]{0:T(512)} %param.9) | copy-start | bytes 6148
  0.0 15.9 %copy-start.1 = (f32[2]{0:T(128)S(1)}, f32[2]{0:T(128)}, u32[]{:S(2)}) copy-start(f32[2]{0:T(128)} %nodes_ref.5) | copy-start | bytes 28
  0.0 15.9 %copy-start.2 = (f32[2]{0:T(128)S(1)}, f32[2]{0:T(128)}, u32[]{:S(2)}) copy-start(f32[2]{0:T(128)} %weights_ref.5) | copy-start | bytes 28
  0.0 15.9 %collective-permute-start = (bf16[1024,512]{1,0:T(8,128)(2,1)}, bf16[1024,512]{1,0:T(8,128)(2,1)S(1)}, u32[]{:S(2)}, u32[]{:S(2)}) collective-permute-start(bf16[1024,512]{1,0:T(8,128)(2,1)} %orb_ref.1), channel_id=1, source_target_pairs={{0,1},{1,0},{2,3},{3,2},{4,5},{5,4},{6,7},{7,6},{8,9},{9,8},{10,11... | collective-permute-start | bytes 3145736 | tf_op jit(solution)/shard_map/ppermute | solution.py:280
  1.4 17.8 %collective-permute-start.1 = (bf16[1024,512]{1,0:T(8,128)(2,1)}, bf16[1024,512]{1,0:T(8,128)(2,1)S(1)}, u32[]{:S(2)}, u32[]{:S(2)}) collective-permute-start(bf16[1024,512]{1,0:T(8,128)(2,1)} %orb_ref.1), channel_id=1, source_target_pairs={{1,2},{2,1},{3,4},{4,3},{5,6},{6,5},{7,72},{72,7},{9,10},{10,9},{1... | collective-permute-start | bytes 3145736 | tf_op jit(solution)/shard_map/ppermute | solution.py:279
